TPU v7x, 256 devices: a whole 4x4x8 slice. The times are simulated.
256 devices in a mesh: grp: 8 (over z_hi, y), dev: 32 (over z_lo, x, core).
Axes of the slice: x: 4, y: 4, z: 8 (z_hi: 2, z_lo: 4; z = z_hi * 4 + z_lo), core: 2. Of those that a mesh axis runs over, the one named last changes fastest.
Arguments:
- series: float32 [2, 1024, 32768], P(None, None, ('grp', 'dev')), may hold values from -6 to 6
- templates: float32 [200, 128], replicated, may hold values from -0.5 to 0.5
- drift_template: int32 [16], replicated, may hold values from 0 to 199
- drift_reach: int32 [16], replicated, may hold values from 4 to 32, as said below
Outputs:
- powers: float32 [16, 33554432], P(None, ('grp', 'dev'))
Inputs may be any that keep to these rules, and one draw needn't show every extreme that they name: Drift d uses the taps t with 32 - drift_reach[d] <= t < 32 + drift_reach[d]; some drift uses all 64 taps.
All inputs are finite; a program needn't handle non-finite values.
Results may differ from a plain program's by a relative error of at most 0.000078.
Values sent between devices are 32-bit elements; how exact they have to be, the bound alone decides.
A program may use at most 64 MiB of HBM per device.

v0:
```python
import functools
import math

import jax
import jax.numpy as jnp
import ml_dtypes
import numpy as np
from jax import lax
from jax.experimental import pallas as pl
from jax.experimental.pallas import tpu as pltpu
from jax.sharding import PartitionSpec as P

N = 67108864
ROWS = 1024
HALF = 256
LANES = 128
TAPS = 64
DRIFTS = 16
DEVICES = 256
MEMBERS = 32
F32 = jnp.float32
BF16 = jnp.bfloat16
MESH = pl.DeviceIdType.MESH


def root(product, length):
    angles = (np.asarray(product, np.int64) % length) * (-2.0 * math.pi / length)
    return np.cos(angles), np.sin(angles)


def halves(table):
    table = np.asarray(table, np.float32)
    high = table.astype(ml_dtypes.bfloat16)
    low = (table - high.astype(np.float32)).astype(ml_dtypes.bfloat16)
    return high, low


@functools.cache
def tables():
    index = np.arange
    done = {}
    cos, sin = root(index(512)[:, None] * index(ROWS)[None, :], ROWS)
    sin[0] = 1.0 - 2.0 * (index(ROWS) % 2)
    column = np.stack([cos, sin]).reshape(2, 2, HALF, ROWS).transpose(1, 0, 2, 3)
    done["column"] = halves(column.reshape(2, 512, ROWS))
    sample = 2 * index(LANES)[None, :] + index(2)[:, None]
    turn = root(sample[:, None, :] * index(512)[None, :, None], N)
    done["turn"] = (np.stack(turn, axis=1) / math.sqrt(N)).astype(np.float32)
    phase = root(2 * LANES * index(DEVICES)[:, None] * index(512)[None, :], N)
    done["phase"] = np.stack(phase, axis=1).reshape(DEVICES, 8, LANES).astype(np.float32)
    middle = root(512 * (2 * LANES * index(HALF)[None, :, None] + sample[:, None, :]), N)
    done["middle"] = np.stack(middle, axis=1).astype(np.float32)
    cos, sin = root(index(HALF)[:, None] * index(HALF)[None, :], HALF)
    done["outer"] = halves(np.block([[cos, -sin], [sin, cos]]))
    twist = root(index(HALF)[:, None] * index(LANES)[None, :], HALF * LANES)
    done["twist"] = np.stack(twist).astype(np.float32)
    cos, sin = root(index(LANES)[:, None] * index(LANES)[None, :], LANES)
    back = slice(None, None, -1)
    done["inner"] = halves(np.block([[cos, -sin], [sin, cos], [cos[back], -sin[back]], [sin[back], cos[back]]]))
    join = np.stack(root(index(HALF)[None, :] + HALF * index(LANES)[:, None], 2 * HALF * LANES))
    done["join"] = np.concatenate([join, join[:, back]]).astype(np.float32)
    order = np.zeros((512, 512), np.float32)
    for row in range(512):
        source = 512 - row
        order[row, source if row else 0] = 1.0
    done["order"] = order.astype(ml_dtypes.bfloat16)
    edge = np.zeros((64, 64), np.float32)
    for row in range(64):
        edge[row, row // 32 * 32 + 31 - row % 32] = 1.0
    done["edge"] = edge.astype(ml_dtypes.bfloat16)
    done["mirror"] = np.eye(LANES, dtype=np.float32)[back].astype(ml_dtypes.bfloat16)
    return done


def split(value):
    high = value.astype(BF16)
    return high, (value - high.astype(F32)).astype(BF16)


def product(left, right):
    dot = functools.partial(jnp.dot, preferred_element_type=F32)
    return dot(left[0], right[0]) + (dot(left[0], right[1]) + dot(left[1], right[0]))


def product_t(left, right):
    def dot(a, b):
        return lax.dot_general(a, b, (((1,), (1,)), ((), ())), preferred_element_type=F32)

    return dot(left[0], right[0]) + (dot(left[0], right[1]) + dot(left[1], right[0]))


def place(target):
    return (target // MEMBERS, lax.rem(target, MEMBERS))


def spectrum_kernel(
    series_in, column_hi_in, column_lo_in, turn_in, phase_in, middle_in, outer_hi_in, outer_lo_in,
    twist_in, inner_hi_in, inner_lo_in, join_in, templates, chosen, reach,
    bins, halo, bands,
    series, column_hi, column_lo, turn, phase, middle, outer_hi, outer_lo, twist, inner_hi, inner_lo, join,
    send_one, recv_one, send_two, edge_out, edge_in,
    load_sem, own_sem, send_sem, recv_sem, edge_send_sem, edge_recv_sem,
):
    me = lax.axis_index("grp") * MEMBERS + lax.axis_index("dev")
    pairs = [
        (series_in, series), (column_hi_in, column_hi), (column_lo_in, column_lo), (turn_in, turn),
        (phase_in.at[me], phase), (middle_in, middle), (outer_hi_in, outer_hi), (outer_lo_in, outer_lo),
        (twist_in, twist), (inner_hi_in, inner_hi), (inner_lo_in, inner_lo), (join_in, join),
    ]
    loads = [pltpu.make_async_copy(a, b, load_sem.at[i]) for i, (a, b) in enumerate(pairs)]
    for load in loads:
        load.start()

    barrier = pltpu.get_barrier_semaphore()

    def greet(step, carry):
        target = place(lax.rem(me + step, DEVICES))
        pl.semaphore_signal(barrier, inc=1, device_id=target, device_id_type=MESH)
        return carry

    lax.fori_loop(1, DEVICES, greet, 0, unroll=5)
    for load in loads:
        load.wait()

    high, low = split(jnp.concatenate([series[0], series[1]], axis=1))
    padded = jnp.concatenate([phase[...]] * 16, axis=0)
    phase_columns = jnp.transpose(padded)

    def column_part(chunk):
        def rows(part):
            at = pl.ds(part * HALF, HALF)
            return product((column_hi[chunk, at, :], column_lo[chunk, at, :]), (high, low))

        real, imag = rows(0), rows(1)
        blocks = (2 * chunk, 2 * chunk + 1)
        phase_real = jnp.concatenate([phase_columns[:, b : b + 1] for b in blocks], axis=0)
        phase_imag = jnp.concatenate([phase_columns[:, b + 4 : b + 5] for b in blocks], axis=0)
        for e in range(2):
            turn_real = turn[e, 0, pl.ds(chunk * HALF, HALF), :]
            turn_imag = turn[e, 1, pl.ds(chunk * HALF, HALF), :]
            full_real = turn_real * phase_real - turn_imag * phase_imag
            full_imag = turn_real * phase_imag + turn_imag * phase_real
            a, b = real[:, e * LANES : (e + 1) * LANES], imag[:, e * LANES : (e + 1) * LANES]
            send_one[chunk, pl.ds(2 * e, HALF, stride=4), :] = a * full_real - b * full_imag
            send_one[chunk, pl.ds(2 * e + 1, HALF, stride=4), :] = a * full_imag + b * full_real

    def send_all(source, target_ref, chunk, number):
        mine = pl.ds(pl.multiple_of(4 * me, 4), 4)
        own = pltpu.make_async_copy(source.at[chunk, mine], target_ref.at[chunk, mine], own_sem.at[number])
        own.start()

        def send(step, carry):
            target = lax.rem(me + step, DEVICES)
            pltpu.make_async_remote_copy(
                src_ref=source.at[chunk, pl.ds(pl.multiple_of(4 * target, 4), 4)],
                dst_ref=target_ref.at[chunk, mine],
                send_sem=send_sem.at[number],
                recv_sem=recv_sem.at[number],
                device_id=place(target),
                device_id_type=MESH,
            ).start()
            return carry

        lax.fori_loop(1, DEVICES, send, 0, unroll=5)
        own.wait()

    def wait_all(source, target_ref, chunk, sem):
        others = pl.ds(0, 4 * (DEVICES - 1))
        pltpu.make_async_copy(source.at[chunk, others], target_ref.at[chunk, others], sem).wait()

    column_part(0)
    pl.semaphore_wait(barrier, DEVICES - 1)
    send_all(send_one, recv_one, 0, 0)
    column_part(1)
    send_all(send_one, recv_one, 1, 1)

    lane = lax.broadcasted_iota(jnp.int32, (1, LANES), 1)
    for d in range(DRIFTS):
        taps = templates[pl.ds(chosen[d], 1), :]
        tap = lax.rem(lane, TAPS)
        inside = (tap >= TAPS // 2 - reach[d]) & (tap < TAPS // 2 + reach[d])
        taps = jnp.where(inside, taps, 0.0)
        real = jnp.where(lane < TAPS, taps, 0.0)
        imag = jnp.where(lane < TAPS, pltpu.roll(taps, TAPS, 1), 0.0)
        band_real = pltpu.roll(jnp.broadcast_to(real, (TAPS, LANES)), 0, 1, stride=1, stride_axis=0)
        band_imag = pltpu.roll(jnp.broadcast_to(imag, (TAPS, LANES)), 0, 1, stride=1, stride_axis=0)
        for part, wide in enumerate(([band_real, -band_imag], [band_imag, band_real])):
            for level, value in enumerate(split(jnp.concatenate(wide, axis=1))):
                bands[level, d // 2, pl.ds(part * LANES + d % 2 * TAPS, TAPS), :] = value

    def row_part(real, imag):
        wide = product((outer_hi[...], outer_lo[...]), split(jnp.concatenate([real, imag], axis=0)))
        done = []
        for e in range(2):
            a, b = wide[:HALF, e * LANES : (e + 1) * LANES], wide[HALF:, e * LANES : (e + 1) * LANES]
            turned = [a * twist[0] - b * twist[1], a * twist[1] + b * twist[0]]
            done.append(
                product_t((inner_hi[...], inner_lo[...]), split(jnp.concatenate(turned, axis=1)))
            )
        return done

    def store(chunk, part, value, flip):
        for h in range(2):
            first = 4 * (1 - h if flip else h) + part
            send_two[chunk, pl.ds(first, LANES, stride=8), :] = value[:, h * LANES : (h + 1) * LANES]

    def store_direct(chunk, even, odd):
        odd_real, odd_imag = odd[0:128], odd[128:256]
        store(chunk, 0, even[0:128] + (join[0] * odd_real - join[1] * odd_imag), False)
        store(chunk, 1, even[128:256] + (join[0] * odd_imag + join[1] * odd_real), False)

    def store_mirrored(chunk, even, odd):
        odd_real, odd_imag = odd[256:384], odd[384:512]
        store(chunk, 2, even[256:384] - (join[2] * odd_real - join[3] * odd_imag), True)
        store(chunk, 3, (join[2] * odd_imag + join[3] * odd_real) - even[384:512], True)

    def arrived(chunk):
        return [recv_one[chunk, pl.ds(s, HALF, stride=4), :] for s in range(4)]

    def rows_of(chunk):
        parts = arrived(chunk)
        real = jnp.concatenate([parts[0], parts[2]], axis=1)
        imag = jnp.concatenate([parts[1], parts[3]], axis=1)
        if chunk == 0:
            imag = imag * (me != 0).astype(F32)
        even, odd = row_part(real, imag)
        store_direct(chunk, even, odd)
        store_mirrored(chunk, even, odd)

    wait_all(send_one, recv_one, 0, recv_sem.at[0])
    rows_of(0)

    @pl.when(me == 0)
    def _():
        parts = arrived(0)
        real = jnp.concatenate([parts[1] * middle[0, 0], parts[3] * middle[1, 0]], axis=1)
        imag = jnp.concatenate([parts[1] * middle[0, 1], parts[3] * middle[1, 1]], axis=1)
        even, odd = row_part(real, imag)
        store_mirrored(0, even, odd)

    send_all(send_two, bins, 0, 2)
    wait_all(send_one, recv_one, 1, recv_sem.at[1])
    rows_of(1)
    send_all(send_two, bins, 1, 3)
    wait_all(send_two, bins, 0, recv_sem.at[2])

    def edge_rows(side):
        first = (4 + 2, 0)[side]
        return jnp.concatenate([bins[0, pl.ds(first + part, 32, stride=4), :] for part in range(2)], axis=0)

    last = DEVICES - 1
    near = [lax.rem(me + 1, DEVICES), lax.rem(me + last, DEVICES)]
    sends = [me < last, me > 0]
    gets = [me > 0, me < last]
    copies = []
    for side in range(2):
        edge_out[side] = edge_rows(side)
        edge_in[side] = jnp.zeros((64, LANES), F32)
    for side in range(2):
        copy = pltpu.make_async_remote_copy(
            src_ref=edge_out.at[side],
            dst_ref=edge_in.at[2 + side],
            send_sem=edge_send_sem.at[side],
            recv_sem=edge_recv_sem.at[side],
            device_id=place(near[side]),
            device_id_type=MESH,
        )
        pl.when(sends[side])(copy.start)
        copies.append(copy)
    first_lane = lax.broadcasted_iota(jnp.int32, (64, LANES), 1) == 0
    for side in range(2):
        pl.when(gets[side])(copies[side].wait_recv)

        @pl.when(gets[side])
        def _():
            edge_in[side] = edge_in[2 + side]

        halo[side] = pltpu.roll(jnp.where(first_lane, edge_in[side], edge_out[side]), LANES - 1, 1)
        pl.when(sends[side])(copies[side].wait_send)

    wait_all(send_two, bins, 1, recv_sem.at[3])
    for number, source, target_ref in ((0, send_one, recv_one), (1, send_one, recv_one), (2, send_two, bins), (3, send_two, bins)):
        wait_all(source, target_ref, number % 2, send_sem.at[number])


def correlate_kernel(bins, halo, order, edge, mirror, bands, out, rows):
    step = pl.program_id(0)

    @pl.when(step == 0)
    def _():
        def flip(value):
            return jnp.dot(value.astype(BF16), mirror[...], preferred_element_type=F32).astype(BF16)

        for part in range(2):
            direct = jnp.concatenate([bins[c, pl.ds(part, HALF, stride=4), :] for c in range(2)], axis=0)
            for level, value in enumerate(split(direct)):
                rows[2 * level + part, pl.ds(32, 512), :] = value
            for level, value in enumerate(split(halo[1, pl.ds(32 * part, 32), :])):
                rows[2 * level + part, pl.ds(1056, 32), :] = value
            mirrored = jnp.concatenate([bins[c, pl.ds(2 + part, HALF, stride=4), :] for c in range(2)], axis=0)
            moved = jnp.dot(order[...], jnp.concatenate(split(mirrored), axis=1), preferred_element_type=F32)
            for level in range(2):
                rows[2 * level + part, pl.ds(544, 512), :] = flip(moved[:, level * LANES : (level + 1) * LANES])
        moved = jnp.dot(edge[...], jnp.concatenate(split(halo[0]), axis=1), preferred_element_type=F32)
        for level in range(2):
            flipped = flip(moved[:, level * LANES : (level + 1) * LANES])
            for part in range(2):
                rows[2 * level + part, pl.ds(0, 32), :] = flipped[32 * part : 32 * part + 32]

    def window(level, odd):
        at = pl.ds(pl.multiple_of(step * LANES + odd * TAPS, TAPS), LANES)
        return jnp.concatenate([jnp.transpose(rows[2 * level + part, at, :]) for part in range(2)], axis=1)

    windows = [jnp.concatenate([window(level, odd) for odd in range(2)], axis=0) for level in range(2)]
    flat = out.reshape(2 * LANES * 8, LANES)
    low_lanes = lax.broadcasted_iota(jnp.int32, (LANES, LANES), 1) < TAPS
    for pair in range(DRIFTS // 2):
        response = product_t(windows, (bands[0, pair], bands[1, pair]))
        real, imag = response[:, :LANES], response[:, LANES:]
        power = real * real + imag * imag
        even, odd = power[:LANES], power[LANES:]
        first = jnp.where(low_lanes, even, pltpu.roll(odd, TAPS, 1))
        second = jnp.where(low_lanes, pltpu.roll(even, TAPS, 1), odd)
        for d, value in ((2 * pair, first), (2 * pair + 1, second)):
            flat[pl.ds(d // 8 * 1024 + d % 8, LANES, stride=8), :] = value


def spectrum(series, templates, drift_template, drift_reach):
    made = tables()
    inputs = [series, *made["column"], made["turn"], made["phase"], made["middle"], *made["outer"], made["twist"], *made["inner"], made["join"]]
    inputs = [jnp.asarray(value) for value in inputs]
    shapes = [value.shape for value in inputs]
    shapes[4] = (8, LANES)
    copies = [pltpu.VMEM(shape, value.dtype) for shape, value in zip(shapes, inputs)]
    chunked = pltpu.VMEM((2, 4 * DEVICES, LANES), F32)
    far = pl.BlockSpec(memory_space=pltpu.HBM)
    vmem = pl.BlockSpec(memory_space=pltpu.VMEM)
    smem = pl.BlockSpec(memory_space=pltpu.SMEM)
    dma = pltpu.SemaphoreType.DMA
    return pl.pallas_call(
        spectrum_kernel,
        name="spectrum",
        out_shape=(
            jax.ShapeDtypeStruct((2, 4 * DEVICES, LANES), F32),
            jax.ShapeDtypeStruct((2, 64, LANES), F32),
            jax.ShapeDtypeStruct((2, DRIFTS // 2, 256, 256), BF16),
        ),
        in_specs=[far] * len(inputs) + [vmem, smem, smem],
        out_specs=(vmem, vmem, vmem),
        scratch_shapes=[
            *copies, chunked, chunked, chunked,
            pltpu.VMEM((2, 64, LANES), F32), pltpu.VMEM((4, 64, LANES), F32),
            dma((len(inputs),)), dma((4,)), dma((4,)), dma((4,)), dma((2,)), dma((2,)),
        ],
        compiler_params=pltpu.CompilerParams(
            collective_id=0, has_side_effects=True, vmem_limit_bytes=60 << 20
        ),
    )(*inputs, templates, drift_template, drift_reach)


def correlate(bins, halo, bands):
    made = tables()
    shifts = [jnp.asarray(made[name]) for name in ("order", "edge", "mirror")]
    vmem = pl.BlockSpec(memory_space=pltpu.VMEM)
    powers = pl.pallas_call(
        correlate_kernel,
        name="correlate",
        grid=(8,),
        out_shape=jax.ShapeDtypeStruct((2, LANES, 8, 8, LANES), F32),
        in_specs=[vmem] * 6,
        out_specs=pl.BlockSpec((2, LANES, 1, 8, LANES), lambda h: (0, 0, h, 0, 0)),
        scratch_shapes=[pltpu.VMEM((4, 1088, LANES), BF16)],
        compiler_params=pltpu.CompilerParams(vmem_limit_bytes=32 << 20),
    )(bins, halo, *shifts, bands)
    return powers.transpose(0, 3, 1, 2, 4).reshape(DRIFTS, LANES * ROWS)


def local(series, templates, drift_template, drift_reach):
    bins, halo, bands = spectrum(series, templates, drift_template, drift_reach)
    return correlate(bins, halo, bands)


def solution(mesh):
    return jax.shard_map(
        local,
        mesh=mesh,
        in_specs=(P(None, None, ("grp", "dev")), P(), P(), P()),
        out_specs=P(None, ("grp", "dev")),
        check_vma=False,
    )
```

profile of v0, /device:TPU:1, one launch (start us, length us, event | category | flops | bytes accessed | tf_op | source)
XLA Modules:
  0.0 81.5 jit_solution(5394810849342855649)
XLA Ops:
  0.0 0.0 copy-start.2
  0.0 0.0 copy-start.4
  0.0 0.0 copy-start.5
  0.0 66.9 %spectrum.1 = (f32[2,1024,128]{2,1,0:T(8,128)}, f32[2,64,128]{2,1,0:T(8,128)}, bf16[2,8,256,256]{3,2,1,0:T(8,128)(2,1)}) custom-call(f32[2,1024,128]{2,1,0:T(8,128)} %series_in.1, bf16[2,512,1024]{2,1,0:T(8,128)(2,1)} %constant.28.clone.column_hi_in, bf16[2,512,1024]{2,1,0:T(8,128)(2,1)} %constant.29.clone.column_lo_in, ...), custom_call_target="tpu_custom_call" | custom-call | tf_op jit(solution)/shard_map/spectrum/pallas_call | solution.py:340
  66.9 0.0 copy-done.2
  66.9 0.0 copy-done.4
  66.9 0.0 copy-done.5
  66.9 0.0 copy-start
  66.9 1.6 %copy-done = bf16[2,8,256,256]{3,2,1,0:T(8,128)(2,1)S(1)} copy-done((bf16[2,8,256,256]{3,2,1,0:T(8,128)(2,1)S(1)}, bf16[2,8,256,256]{3,2,1,0:T(8,128)(2,1)}, u32[]{:S(2)}) %copy-start) | copy-done | bytes 2097176
  68.5 0.0 copy-start.1
  68.5 1.2 %copy-done.1 = f32[2,1024,128]{2,1,0:T(8,128)S(1)} copy-done((f32[2,1024,128]{2,1,0:T(8,128)S(1)}, f32[2,1024,128]{2,1,0:T(8,128)}, u32[]{:S(2)}) %copy-start.1) | copy-done | bytes 1048600
  69.7 0.0 copy-start.3
  69.7 0.8 %copy-done.3 = f32[2,64,128]{2,1,0:T(8,128)S(1)} copy-done((f32[2,64,128]{2,1,0:T(8,128)S(1)}, f32[2,64,128]{2,1,0:T(8,128)}, u32[]{:S(2)}) %copy-start.3) | copy-done | bytes 65560
  70.6 10.9 %correlate.1 = f32[2,128,8,8,128]{4,3,2,1,0:T(8,128)} custom-call(f32[2,1024,128]{2,1,0:T(8,128)S(1)} %copy-done.1, f32[2,64,128]{2,1,0:T(8,128)S(1)} %copy-done.3, bf16[512,512]{1,0:T(8,128)(2,1)S(1)} %copy-done.2, bf16[64,64]{1,0:T(8,128)(2,1)S(1)} %copy-done.5, bf16[128,128]{1,0:T(8,128)(2,1)S(1)} %copy-done.4, bf16[2,8,256,256]{3,2,1,0:T(8,128)(2,1)S(1)} %copy-done), custom_call_target="tpu_custom_call" | custom-call | tf_op jit(solution)/shard_map/correlate/pallas_call | solution.py:365
Async XLA Ops:
  0.0 66.9 %copy-start.2 = (bf16[512,512]{1,0:T(8,128)(2,1)S(1)}, bf16[512,512]{1,0:T(8,128)(2,1)}, u32[]{:S(2)}) copy-start(bf16[512,512]{1,0:T(8,128)(2,1)} %constant.39.clone.order) | copy-start | bytes 1572868
  0.0 66.9 %copy-start.4 = (bf16[128,128]{1,0:T(8,128)(2,1)S(1)}, bf16[128,128]{1,0:T(8,128)(2,1)}, u32[]{:S(2)}) copy-start(bf16[128,128]{1,0:T(8,128)(2,1)} %constant.41.clone.mirror) | copy-start | bytes 98308
  0.0 66.9 %copy-start.5 = (bf16[64,64]{1,0:T(8,128)(2,1)S(1)}, bf16[64,64]{1,0:T(8,128)(2,1)}, u32[]{:S(2)}) copy-start(bf16[64,64]{1,0:T(8,128)(2,1)} %constant.40.clone.edge) | copy-start | bytes 24580
  66.9 1.6 %copy-start = (bf16[2,8,256,256]{3,2,1,0:T(8,128)(2,1)S(1)}, bf16[2,8,256,256]{3,2,1,0:T(8,128)(2,1)}, u32[]{:S(2)}) copy-start(bf16[2,8,256,256]{3,2,1,0:T(8,128)(2,1)} %get-tuple-element.10.bands) | copy-start | bytes 6291460
  68.5 1.2 %copy-start.1 = (f32[2,1024,128]{2,1,0:T(8,128)S(1)}, f32[2,1024,128]{2,1,0:T(8,128)}, u32[]{:S(2)}) copy-start(f32[2,1024,128]{2,1,0:T(8,128)} %get-tuple-element.8.bins) | copy-start | bytes 3145732
  69.7 0.8 %copy-start.3 = (f32[2,64,128]{2,1,0:T(8,128)S(1)}, f32[2,64,128]{2,1,0:T(8,128)}, u32[]{:S(2)}) copy-start(f32[2,64,128]{2,1,0:T(8,128)} %get-tuple-element.9.halo) | copy-start | bytes 196612
where the time goes:
time: 81.7 us; the launch traced here: 81.5 us
  Pallas kernels  77.8 us (95%)
  local copies, waits for them, and re-layouts  3.66 us (4%)
    pallas_call x1, Pallas kernels, spectrum(): pl.pallas_call(spectrum_kernel, name='spectrum', out_shape=(jax.ShapeDtyp...  66.9 us
    pallas_call x1, Pallas kernels, correlate(): pl.pallas_call(correlate_kernel, name='correlate', grid=(8,), out_shape=j...  10.9 us
    unnamed x12, local copies, waits for them, and re-layouts  3.66 us

commit v1 on v0

--- a/solution.py
+++ b/solution.py
@@ -18,6 +18,8 @@
 DRIFTS = 16
 DEVICES = 256
 MEMBERS = 32
+GROUPS = 8
+MIDDLE = 832
 F32 = jnp.float32
 BF16 = jnp.bfloat16
 MESH = pl.DeviceIdType.MESH
@@ -95,30 +97,36 @@
 
 def spectrum_kernel(
     series_in, column_hi_in, column_lo_in, turn_in, phase_in, middle_in, outer_hi_in, outer_lo_in,
-    twist_in, inner_hi_in, inner_lo_in, join_in, templates, chosen, reach,
-    bins, halo, bands,
+    twist_in, inner_hi_in, inner_lo_in, join_in, order_in, edge_in, mirror_in, templates, chosen, reach,
+    rows_out, early_out, bands_out,
     series, column_hi, column_lo, turn, phase, middle, outer_hi, outer_lo, twist, inner_hi, inner_lo, join,
-    send_one, recv_one, send_two, edge_out, edge_in,
-    load_sem, own_sem, send_sem, recv_sem, edge_send_sem, edge_recv_sem,
+    order, edge, mirror,
+    send_one, recv_one, send_two, bins, halo_out, halo_in, rows, mixed, early, bands,
+    load_sem, own_sem, send_sem, recv_sem, halo_send_sem, halo_recv_sem, out_sem, ready,
 ):
     me = lax.axis_index("grp") * MEMBERS + lax.axis_index("dev")
     pairs = [
         (series_in, series), (column_hi_in, column_hi), (column_lo_in, column_lo), (turn_in, turn),
         (phase_in.at[me], phase), (middle_in, middle), (outer_hi_in, outer_hi), (outer_lo_in, outer_lo),
         (twist_in, twist), (inner_hi_in, inner_hi), (inner_lo_in, inner_lo), (join_in, join),
+        (order_in, order), (edge_in, edge), (mirror_in, mirror),
     ]
     loads = [pltpu.make_async_copy(a, b, load_sem.at[i]) for i, (a, b) in enumerate(pairs)]
+    def tell(semaphore, size, target):
+        def one(step, carry):
+            pl.semaphore_signal(semaphore, inc=1, device_id=target(step), device_id_type=MESH)
+            return carry
+
+        lax.fori_loop(1, size, one, 0)
+
+    barrier = pltpu.get_barrier_semaphore()
+    group, member = lax.axis_index("grp"), lax.axis_index("dev")
+    tell(barrier, GROUPS, lambda step: (lax.rem(group + step, GROUPS), member))
+    tell(barrier, MEMBERS, lambda step: (group, lax.rem(member + step, MEMBERS)))
     for load in loads:
         load.start()
-
-    barrier = pltpu.get_barrier_semaphore()
-
-    def greet(step, carry):
-        target = place(lax.rem(me + step, DEVICES))
-        pl.semaphore_signal(barrier, inc=1, device_id=target, device_id_type=MESH)
-        return carry
-
-    lax.fori_loop(1, DEVICES, greet, 0, unroll=5)
+    pl.semaphore_wait(barrier, GROUPS + MEMBERS - 2)
+    tell(ready, MEMBERS, lambda step: (group, lax.rem(member + step, MEMBERS)))
     for load in loads:
         load.wait()
 
@@ -169,7 +177,7 @@
         pltpu.make_async_copy(source.at[chunk, others], target_ref.at[chunk, others], sem).wait()
 
     column_part(0)
-    pl.semaphore_wait(barrier, DEVICES - 1)
+    pl.semaphore_wait(ready, MEMBERS - 1)
     send_all(send_one, recv_one, 0, 0)
     column_part(1)
     send_all(send_one, recv_one, 1, 1)
@@ -186,7 +194,10 @@
         band_imag = pltpu.roll(jnp.broadcast_to(imag, (TAPS, LANES)), 0, 1, stride=1, stride_axis=0)
         for part, wide in enumerate(([band_real, -band_imag], [band_imag, band_real])):
             for level, value in enumerate(split(jnp.concatenate(wide, axis=1))):
-                bands[level, d // 2, pl.ds(part * LANES + d % 2 * TAPS, TAPS), :] = value
+                bands[d // 2, level, pl.ds(part * LANES + d % 2 * TAPS, TAPS), :] = value
+
+    bands_copy = pltpu.make_async_copy(bands, bands_out, out_sem.at[0])
+    bands_copy.start()
 
     def row_part(real, imag):
         wide = product((outer_hi[...], outer_lo[...]), split(jnp.concatenate([real, imag], axis=0)))
@@ -244,7 +255,7 @@
     send_all(send_two, bins, 1, 3)
     wait_all(send_two, bins, 0, recv_sem.at[2])
 
-    def edge_rows(side):
+    def halo_rows(side):
         first = (4 + 2, 0)[side]
         return jnp.concatenate([bins[0, pl.ds(first + part, 32, stride=4), :] for part in range(2)], axis=0)
 
@@ -254,103 +265,164 @@
     gets = [me > 0, me < last]
     copies = []
     for side in range(2):
-        edge_out[side] = edge_rows(side)
-        edge_in[side] = jnp.zeros((64, LANES), F32)
+        halo_out[side] = halo_rows(side)
+        halo_in[side] = jnp.zeros((64, LANES), F32)
     for side in range(2):
         copy = pltpu.make_async_remote_copy(
-            src_ref=edge_out.at[side],
-            dst_ref=edge_in.at[2 + side],
-            send_sem=edge_send_sem.at[side],
-            recv_sem=edge_recv_sem.at[side],
+            src_ref=halo_out.at[side],
+            dst_ref=halo_in.at[2 + side],
+            send_sem=halo_send_sem.at[side],
+            recv_sem=halo_recv_sem.at[side],
             device_id=place(near[side]),
             device_id_type=MESH,
         )
         pl.when(sends[side])(copy.start)
         copies.append(copy)
+
+    def flip(value):
+        return jnp.dot(value.astype(BF16), mirror[...], preferred_element_type=F32).astype(BF16)
+
+    def put_direct(chunk):
+        for part in range(2):
+            for level, value in enumerate(split(bins[chunk, pl.ds(part, HALF, stride=4), :])):
+                rows[2 * level + part, pl.ds(32 + HALF * chunk, HALF), :] = value
+            wide = jnp.concatenate(split(bins[chunk, pl.ds(2 + part, HALF, stride=4), :]), axis=1)
+            mixed[pl.ds(HALF * chunk, HALF), pl.ds(2 * LANES * part, 2 * LANES)] = wide
+
+    def put_mirrored(moved, first, count):
+        for part in range(2):
+            for level in range(2):
+                at = (2 * part + level) * LANES
+                rows[2 * level + part, pl.ds(first, count), :] = flip(moved[:, at : at + LANES])
+
+    put_direct(0)
+    moved = jnp.dot(order[pl.ds(HALF, HALF), pl.ds(0, HALF)], mixed[pl.ds(0, HALF), :], preferred_element_type=F32)
+    put_mirrored(moved, 800, HALF)
+
     first_lane = lax.broadcasted_iota(jnp.int32, (64, LANES), 1) == 0
+    sides = []
     for side in range(2):
         pl.when(gets[side])(copies[side].wait_recv)
 
         @pl.when(gets[side])
         def _():
-            edge_in[side] = edge_in[2 + side]
-
-        halo[side] = pltpu.roll(jnp.where(first_lane, edge_in[side], edge_out[side]), LANES - 1, 1)
+            halo_in[side] = halo_in[2 + side]
+
+        sides.append(split(pltpu.roll(jnp.where(first_lane, halo_in[side], halo_out[side]), LANES - 1, 1)))
         pl.when(sends[side])(copies[side].wait_send)
+    moved = jnp.dot(edge[...], jnp.concatenate(sides[0], axis=1), preferred_element_type=F32)
+    for level in range(2):
+        flipped = flip(moved[:, level * LANES : (level + 1) * LANES])
+        for part in range(2):
+            rows[2 * level + part, pl.ds(0, 32), :] = flipped[32 * part : 32 * part + 32]
+            rows[2 * level + part, pl.ds(1056, 32), :] = sides[1][level][32 * part : 32 * part + 32]
+
+    correlate_tiles(rows, bands, [0, 14 * TAPS], early.reshape(2 * LANES * 2 * 8, LANES), lambda pair: None)
+    early_copy = pltpu.make_async_copy(early, early_out, out_sem.at[1])
+    early_copy.start()
 
     wait_all(send_two, bins, 1, recv_sem.at[3])
-    for number, source, target_ref in ((0, send_one, recv_one), (1, send_one, recv_one), (2, send_two, bins), (3, send_two, bins)):
+    put_direct(1)
+    moved = jnp.dot(order[pl.ds(0, 272), :], mixed[...], preferred_element_type=F32)
+    put_mirrored(moved, 544, 272)
+    rows_copy = pltpu.make_async_copy(rows.at[:, pl.ds(LANES, MIDDLE)], rows_out, out_sem.at[2])
+    rows_copy.start()
+    for number, source, target_ref in (
+        (0, send_one, recv_one), (1, send_one, recv_one), (2, send_two, bins), (3, send_two, bins)
+    ):
         wait_all(source, target_ref, number % 2, send_sem.at[number])
-
-
-def correlate_kernel(bins, halo, order, edge, mirror, bands, out, rows):
-    step = pl.program_id(0)
-
-    @pl.when(step == 0)
-    def _():
-        def flip(value):
-            return jnp.dot(value.astype(BF16), mirror[...], preferred_element_type=F32).astype(BF16)
-
-        for part in range(2):
-            direct = jnp.concatenate([bins[c, pl.ds(part, HALF, stride=4), :] for c in range(2)], axis=0)
-            for level, value in enumerate(split(direct)):
-                rows[2 * level + part, pl.ds(32, 512), :] = value
-            for level, value in enumerate(split(halo[1, pl.ds(32 * part, 32), :])):
-                rows[2 * level + part, pl.ds(1056, 32), :] = value
-            mirrored = jnp.concatenate([bins[c, pl.ds(2 + part, HALF, stride=4), :] for c in range(2)], axis=0)
-            moved = jnp.dot(order[...], jnp.concatenate(split(mirrored), axis=1), preferred_element_type=F32)
-            for level in range(2):
-                rows[2 * level + part, pl.ds(544, 512), :] = flip(moved[:, level * LANES : (level + 1) * LANES])
-        moved = jnp.dot(edge[...], jnp.concatenate(split(halo[0]), axis=1), preferred_element_type=F32)
-        for level in range(2):
-            flipped = flip(moved[:, level * LANES : (level + 1) * LANES])
-            for part in range(2):
-                rows[2 * level + part, pl.ds(0, 32), :] = flipped[32 * part : 32 * part + 32]
-
-    def window(level, odd):
-        at = pl.ds(pl.multiple_of(step * LANES + odd * TAPS, TAPS), LANES)
+    bands_copy.wait()
+    early_copy.wait()
+    rows_copy.wait()
+
+
+def correlate_tiles(rows, bands, starts, flat, before):
+    def window(level, first):
+        at = pl.ds(first, LANES)
         return jnp.concatenate([jnp.transpose(rows[2 * level + part, at, :]) for part in range(2)], axis=1)
 
-    windows = [jnp.concatenate([window(level, odd) for odd in range(2)], axis=0) for level in range(2)]
-    flat = out.reshape(2 * LANES * 8, LANES)
+    count = len(starts)
+    firsts = [start + odd * TAPS for start in starts for odd in range(2)]
+    windows = [jnp.concatenate([window(level, first) for first in firsts], axis=0) for level in range(2)]
     low_lanes = lax.broadcasted_iota(jnp.int32, (LANES, LANES), 1) < TAPS
     for pair in range(DRIFTS // 2):
-        response = product_t(windows, (bands[0, pair], bands[1, pair]))
+        before(pair)
+        response = product_t(windows, (bands[pair, 0], bands[pair, 1]))
         real, imag = response[:, :LANES], response[:, LANES:]
         power = real * real + imag * imag
-        even, odd = power[:LANES], power[LANES:]
-        first = jnp.where(low_lanes, even, pltpu.roll(odd, TAPS, 1))
-        second = jnp.where(low_lanes, pltpu.roll(even, TAPS, 1), odd)
-        for d, value in ((2 * pair, first), (2 * pair + 1, second)):
-            flat[pl.ds(d // 8 * 1024 + d % 8, LANES, stride=8), :] = value
+        for tile in range(count):
+            even = power[2 * LANES * tile : 2 * LANES * tile + LANES]
+            odd = power[2 * LANES * tile + LANES : 2 * LANES * (tile + 1)]
+            first = jnp.where(low_lanes, even, pltpu.roll(odd, TAPS, 1))
+            second = jnp.where(low_lanes, pltpu.roll(even, TAPS, 1), odd)
+            for d, value in ((2 * pair, first), (2 * pair + 1, second)):
+                at = (d // 8 * LANES * count + tile) * 8 + d % 8
+                flat[pl.ds(at, LANES, stride=8 * count), :] = value
+
+
+def correlate_kernel(rows_in, early_in, bands_in, out, rows, bands, *rest):
+    tiles, (row_sem, band_sem, early_sem, out_sem) = rest[:6], rest[6:]
+    row_copy = pltpu.make_async_copy(rows_in, rows, row_sem)
+    row_copy.start()
+    band_copies = []
+    for pair in range(DRIFTS // 2):
+        copy = pltpu.make_async_copy(bands_in.at[pair], bands.at[pair], band_sem.at[pair])
+        copy.start()
+        band_copies.append(copy)
+    copies = []
+    for slot, tile in enumerate((0, 7)):
+        copy = pltpu.make_async_copy(early_in.at[:, :, slot], out.at[:, :, tile], early_sem.at[slot])
+        copy.start()
+        copies.append(copy)
+    row_copy.wait()
+    for tile in range(1, 7):
+        held = tiles[tile - 1]
+
+        def before(pair):
+            if tile == 1:
+                band_copies[pair].wait()
+
+        correlate_tiles(rows, bands, [(tile - 1) * LANES], held.reshape(2 * LANES * 8, LANES), before)
+        copy = pltpu.make_async_copy(held, out.at[:, :, tile], out_sem.at[tile - 1])
+        copy.start()
+        copies.append(copy)
+    for copy in copies:
+        copy.wait()
 
 
 def spectrum(series, templates, drift_template, drift_reach):
     made = tables()
-    inputs = [series, *made["column"], made["turn"], made["phase"], made["middle"], *made["outer"], made["twist"], *made["inner"], made["join"]]
+    inputs = [
+        series, *made["column"], made["turn"], made["phase"], made["middle"], *made["outer"],
+        made["twist"], *made["inner"], made["join"], made["order"], made["edge"], made["mirror"],
+    ]
     inputs = [jnp.asarray(value) for value in inputs]
     shapes = [value.shape for value in inputs]
     shapes[4] = (8, LANES)
     copies = [pltpu.VMEM(shape, value.dtype) for shape, value in zip(shapes, inputs)]
     chunked = pltpu.VMEM((2, 4 * DEVICES, LANES), F32)
-    far = pl.BlockSpec(memory_space=pltpu.HBM)
-    vmem = pl.BlockSpec(memory_space=pltpu.VMEM)
+    far = pl.BlockSpec(memory_space=pl.ANY)
     smem = pl.BlockSpec(memory_space=pltpu.SMEM)
     dma = pltpu.SemaphoreType.DMA
+    early = (2, LANES, 2, 8, LANES)
+    bands = (DRIFTS // 2, 2, 256, 256)
     return pl.pallas_call(
         spectrum_kernel,
         name="spectrum",
         out_shape=(
-            jax.ShapeDtypeStruct((2, 4 * DEVICES, LANES), F32),
-            jax.ShapeDtypeStruct((2, 64, LANES), F32),
-            jax.ShapeDtypeStruct((2, DRIFTS // 2, 256, 256), BF16),
+            jax.ShapeDtypeStruct((4, MIDDLE, LANES), BF16),
+            jax.ShapeDtypeStruct(early, F32),
+            jax.ShapeDtypeStruct(bands, BF16),
         ),
-        in_specs=[far] * len(inputs) + [vmem, smem, smem],
-        out_specs=(vmem, vmem, vmem),
+        in_specs=[far] * len(inputs) + [pl.BlockSpec(memory_space=pltpu.VMEM), smem, smem],
+        out_specs=(far, far, far),
         scratch_shapes=[
-            *copies, chunked, chunked, chunked,
+            *copies, chunked, chunked, chunked, chunked,
             pltpu.VMEM((2, 64, LANES), F32), pltpu.VMEM((4, 64, LANES), F32),
-            dma((len(inputs),)), dma((4,)), dma((4,)), dma((4,)), dma((2,)), dma((2,)),
+            pltpu.VMEM((4, 1088, LANES), BF16), pltpu.VMEM((512, 512), BF16),
+            pltpu.VMEM(early, F32), pltpu.VMEM(bands, BF16),
+            dma((len(inputs),)), dma((4,)), dma((4,)), dma((4,)), dma((2,)), dma((2,)), dma((3,)),
+            pltpu.SemaphoreType.REGULAR,
         ],
         compiler_params=pltpu.CompilerParams(
             collective_id=0, has_side_effects=True, vmem_limit_bytes=60 << 20
@@ -358,26 +430,27 @@
     )(*inputs, templates, drift_template, drift_reach)
 
 
-def correlate(bins, halo, bands):
-    made = tables()
-    shifts = [jnp.asarray(made[name]) for name in ("order", "edge", "mirror")]
-    vmem = pl.BlockSpec(memory_space=pltpu.VMEM)
+def correlate(rows, early, bands):
+    far = pl.BlockSpec(memory_space=pl.ANY)
+    dma = pltpu.SemaphoreType.DMA
     powers = pl.pallas_call(
         correlate_kernel,
         name="correlate",
-        grid=(8,),
         out_shape=jax.ShapeDtypeStruct((2, LANES, 8, 8, LANES), F32),
-        in_specs=[vmem] * 6,
-        out_specs=pl.BlockSpec((2, LANES, 1, 8, LANES), lambda h: (0, 0, h, 0, 0)),
-        scratch_shapes=[pltpu.VMEM((4, 1088, LANES), BF16)],
-        compiler_params=pltpu.CompilerParams(vmem_limit_bytes=32 << 20),
-    )(bins, halo, *shifts, bands)
+        in_specs=[far] * 3,
+        out_specs=far,
+        scratch_shapes=[
+            pltpu.VMEM(rows.shape, BF16), pltpu.VMEM(bands.shape, BF16),
+            *[pltpu.VMEM((2, LANES, 8, LANES), F32) for _ in range(6)],
+            dma, dma((DRIFTS // 2,)), dma((2,)), dma((6,)),
+        ],
+        compiler_params=pltpu.CompilerParams(vmem_limit_bytes=60 << 20),
+    )(rows, early, bands)
     return powers.transpose(0, 3, 1, 2, 4).reshape(DRIFTS, LANES * ROWS)
 
 
 def local(series, templates, drift_template, drift_reach):
-    bins, halo, bands = spectrum(series, templates, drift_template, drift_reach)
-    return correlate(bins, halo, bands)
+    return correlate(*spectrum(series, templates, drift_template, drift_reach))
 
 
 def solution(mesh):

time: 81.7 us -> 133 us (1.63)
  the two profiles are of different devices: /device:TPU:1 before, /device:TPU:8 now
where the time goes in v1:
time: 133 us
  Pallas kernels  133 us (100%)
    pallas_call x1, Pallas kernels, spectrum(): pl.pallas_call(spectrum_kernel, name='spectrum', out_shape=(jax.ShapeDtyp...  67.9 us
    pallas_call x1, Pallas kernels, correlate(): pl.pallas_call(correlate_kernel, name='correlate', out_shape=jax.ShapeDty...  64.8 us

profile of v1, /device:TPU:8, one launch (start us, length us, event | category | flops | bytes accessed | tf_op | source)
XLA Modules:
  0.0 132.9 jit_solution(1557710328268369634)
XLA Ops:
  0.0 67.9 %spectrum.1 = (bf16[4,832,128]{2,1,0:T(8,128)(2,1)}, f32[2,128,2,8,128]{4,3,2,1,0:T(8,128)}, bf16[8,2,256,256]{3,2,1,0:T(8,128)(2,1)}) custom-call(f32[2,1024,128]{2,1,0:T(8,128)} %series_in.1, bf16[2,512,1024]{2,1,0:T(8,128)(2,1)} %constant.28.clone.column_hi_in, bf16[2,512,1024]{2,1,0:T(8,128)(2,1)} %constant.29.clone.column_lo_in, ...), custom_call_target="tpu_custom_call" | custom-call | tf_op jit(solution)/shard_map/spectrum/pallas_call | solution.py:409
  67.9 64.8 %correlate.1 = f32[2,128,8,8,128]{4,3,2,1,0:T(8,128)} custom-call(bf16[4,832,128]{2,1,0:T(8,128)(2,1)} %get-tuple-element.8.rows_in, f32[2,128,2,8,128]{4,3,2,1,0:T(8,128)} %get-tuple-element.9.early_in, bf16[8,2,256,256]{3,2,1,0:T(8,128)(2,1)} %get-tuple-element.10.bands_in), custom_call_target="tpu_custom_call" | custom-call | tf_op jit(solution)/shard_map/correlate/pallas_call | solution.py:436

commit v2 on v1

--- a/solution.py
+++ b/solution.py
@@ -19,7 +19,7 @@
 DEVICES = 256
 MEMBERS = 32
 GROUPS = 8
-MIDDLE = 832
+EXTENDED = 1088
 F32 = jnp.float32
 BF16 = jnp.bfloat16
 MESH = pl.DeviceIdType.MESH
@@ -98,16 +98,17 @@
 def spectrum_kernel(
     series_in, column_hi_in, column_lo_in, turn_in, phase_in, middle_in, outer_hi_in, outer_lo_in,
     twist_in, inner_hi_in, inner_lo_in, join_in, order_in, edge_in, mirror_in, templates, chosen, reach,
-    rows_out, early_out, bands_out,
+    rows_out, bands_out,
     series, column_hi, column_lo, turn, phase, middle, outer_hi, outer_lo, twist, inner_hi, inner_lo, join,
     order, edge, mirror,
-    send_one, recv_one, send_two, bins, halo_out, halo_in, rows, mixed, early, bands,
+    send_one, recv_one, send_two, bins, halo_out, halo_in, rows, mixed, bands,
     load_sem, own_sem, send_sem, recv_sem, halo_send_sem, halo_recv_sem, out_sem, ready,
 ):
     me = lax.axis_index("grp") * MEMBERS + lax.axis_index("dev")
     pairs = [
-        (series_in, series), (column_hi_in, column_hi), (column_lo_in, column_lo), (turn_in, turn),
-        (phase_in.at[me], phase), (middle_in, middle), (outer_hi_in, outer_hi), (outer_lo_in, outer_lo),
+        (phase_in.at[me], phase), (series_in, series),
+        (column_hi_in.at[0], column_hi.at[0]), (column_lo_in.at[0], column_lo.at[0]), (turn_in, turn),
+        (column_hi_in.at[1], column_hi.at[1]), (column_lo_in.at[1], column_lo.at[1]), (middle_in, middle), (outer_hi_in, outer_hi), (outer_lo_in, outer_lo),
         (twist_in, twist), (inner_hi_in, inner_hi), (inner_lo_in, inner_lo), (join_in, join),
         (order_in, order), (edge_in, edge), (mirror_in, mirror),
     ]
@@ -119,15 +120,17 @@
 
         lax.fori_loop(1, size, one, 0)
 
+    for load in loads[:5]:
+        load.start()
     barrier = pltpu.get_barrier_semaphore()
     group, member = lax.axis_index("grp"), lax.axis_index("dev")
     tell(barrier, GROUPS, lambda step: (lax.rem(group + step, GROUPS), member))
     tell(barrier, MEMBERS, lambda step: (group, lax.rem(member + step, MEMBERS)))
-    for load in loads:
-        load.start()
     pl.semaphore_wait(barrier, GROUPS + MEMBERS - 2)
     tell(ready, MEMBERS, lambda step: (group, lax.rem(member + step, MEMBERS)))
-    for load in loads:
+    for load in loads[5:]:
+        load.start()
+    for load in loads[:5]:
         load.wait()
 
     high, low = split(jnp.concatenate([series[0], series[1]], axis=1))
@@ -179,6 +182,8 @@
     column_part(0)
     pl.semaphore_wait(ready, MEMBERS - 1)
     send_all(send_one, recv_one, 0, 0)
+    for load in loads[5:]:
+        load.wait()
     column_part(1)
     send_all(send_one, recv_one, 1, 1)
 
@@ -317,51 +322,28 @@
             rows[2 * level + part, pl.ds(0, 32), :] = flipped[32 * part : 32 * part + 32]
             rows[2 * level + part, pl.ds(1056, 32), :] = sides[1][level][32 * part : 32 * part + 32]
 
-    correlate_tiles(rows, bands, [0, 14 * TAPS], early.reshape(2 * LANES * 2 * 8, LANES), lambda pair: None)
-    early_copy = pltpu.make_async_copy(early, early_out, out_sem.at[1])
-    early_copy.start()
-
+    def rows_part(number, first, count):
+        at = pl.ds(first, count)
+        copy = pltpu.make_async_copy(rows.at[:, at], rows_out.at[:, at], out_sem.at[number])
+        copy.start()
+        return copy
+
+    rows_copies = [rows_part(1, 0, 288), rows_part(2, 816, 272)]
     wait_all(send_two, bins, 1, recv_sem.at[3])
     put_direct(1)
     moved = jnp.dot(order[pl.ds(0, 272), :], mixed[...], preferred_element_type=F32)
     put_mirrored(moved, 544, 272)
-    rows_copy = pltpu.make_async_copy(rows.at[:, pl.ds(LANES, MIDDLE)], rows_out, out_sem.at[2])
-    rows_copy.start()
+    rows_copies.append(rows_part(3, 288, 528))
     for number, source, target_ref in (
         (0, send_one, recv_one), (1, send_one, recv_one), (2, send_two, bins), (3, send_two, bins)
     ):
         wait_all(source, target_ref, number % 2, send_sem.at[number])
-    bands_copy.wait()
-    early_copy.wait()
-    rows_copy.wait()
-
-
-def correlate_tiles(rows, bands, starts, flat, before):
-    def window(level, first):
-        at = pl.ds(first, LANES)
-        return jnp.concatenate([jnp.transpose(rows[2 * level + part, at, :]) for part in range(2)], axis=1)
-
-    count = len(starts)
-    firsts = [start + odd * TAPS for start in starts for odd in range(2)]
-    windows = [jnp.concatenate([window(level, first) for first in firsts], axis=0) for level in range(2)]
-    low_lanes = lax.broadcasted_iota(jnp.int32, (LANES, LANES), 1) < TAPS
-    for pair in range(DRIFTS // 2):
-        before(pair)
-        response = product_t(windows, (bands[pair, 0], bands[pair, 1]))
-        real, imag = response[:, :LANES], response[:, LANES:]
-        power = real * real + imag * imag
-        for tile in range(count):
-            even = power[2 * LANES * tile : 2 * LANES * tile + LANES]
-            odd = power[2 * LANES * tile + LANES : 2 * LANES * (tile + 1)]
-            first = jnp.where(low_lanes, even, pltpu.roll(odd, TAPS, 1))
-            second = jnp.where(low_lanes, pltpu.roll(even, TAPS, 1), odd)
-            for d, value in ((2 * pair, first), (2 * pair + 1, second)):
-                at = (d // 8 * LANES * count + tile) * 8 + d % 8
-                flat[pl.ds(at, LANES, stride=8 * count), :] = value
-
-
-def correlate_kernel(rows_in, early_in, bands_in, out, rows, bands, *rest):
-    tiles, (row_sem, band_sem, early_sem, out_sem) = rest[:6], rest[6:]
+    for copy in (bands_copy, *rows_copies):
+        copy.wait()
+
+
+def correlate_kernel(rows_in, bands_in, out, rows, bands, *rest):
+    tiles, (row_sem, band_sem, out_sem) = rest[:8], rest[8:]
     row_copy = pltpu.make_async_copy(rows_in, rows, row_sem)
     row_copy.start()
     band_copies = []
@@ -369,23 +351,40 @@
         copy = pltpu.make_async_copy(bands_in.at[pair], bands.at[pair], band_sem.at[pair])
         copy.start()
         band_copies.append(copy)
-    copies = []
-    for slot, tile in enumerate((0, 7)):
-        copy = pltpu.make_async_copy(early_in.at[:, :, slot], out.at[:, :, tile], early_sem.at[slot])
-        copy.start()
-        copies.append(copy)
+
+    def windows_of(tile):
+        def window(level, odd):
+            at = pl.ds(tile * LANES + odd * TAPS, LANES)
+            return jnp.concatenate([jnp.transpose(rows[2 * level + part, at, :]) for part in range(2)], axis=1)
+
+        return [jnp.concatenate([window(level, odd) for odd in range(2)], axis=0) for level in range(2)]
+
+    low_lanes = lax.broadcasted_iota(jnp.int32, (LANES, LANES), 1) < TAPS
+    copies, pending = [], []
     row_copy.wait()
-    for tile in range(1, 7):
-        held = tiles[tile - 1]
-
-        def before(pair):
-            if tile == 1:
-                band_copies[pair].wait()
-
-        correlate_tiles(rows, bands, [(tile - 1) * LANES], held.reshape(2 * LANES * 8, LANES), before)
-        copy = pltpu.make_async_copy(held, out.at[:, :, tile], out_sem.at[tile - 1])
-        copy.start()
-        copies.append(copy)
+    for copy in band_copies:
+        copy.wait()
+    coming = windows_of(0)
+    for tile in range(8):
+        windows = coming
+        if tile < 7:
+            coming = windows_of(tile + 1)
+        flat = tiles[tile].reshape(2 * LANES * 8, LANES)
+        for pair in range(DRIFTS // 2):
+            response = product_t(windows, (bands[pair, 0], bands[pair, 1]))
+            real, imag = response[:, :LANES], response[:, LANES:]
+            power = real * real + imag * imag
+            even, odd = power[:LANES], power[LANES:]
+            first = jnp.where(low_lanes, even, pltpu.roll(odd, TAPS, 1))
+            second = jnp.where(low_lanes, pltpu.roll(even, TAPS, 1), odd)
+            for d, value in ((2 * pair, first), (2 * pair + 1, second)):
+                flat[pl.ds(d // 8 * LANES * 8 + d % 8, LANES, stride=8), :] = value
+        pending.append(pltpu.make_async_copy(tiles[tile], out.at[:, :, tile], out_sem.at[tile]))
+        if tile in (3, 6, 7):
+            for copy in pending:
+                copy.start()
+            copies += pending
+            pending = []
     for copy in copies:
         copy.wait()
 
@@ -404,24 +403,22 @@
     far = pl.BlockSpec(memory_space=pl.ANY)
     smem = pl.BlockSpec(memory_space=pltpu.SMEM)
     dma = pltpu.SemaphoreType.DMA
-    early = (2, LANES, 2, 8, LANES)
     bands = (DRIFTS // 2, 2, 256, 256)
     return pl.pallas_call(
         spectrum_kernel,
         name="spectrum",
         out_shape=(
-            jax.ShapeDtypeStruct((4, MIDDLE, LANES), BF16),
-            jax.ShapeDtypeStruct(early, F32),
+            jax.ShapeDtypeStruct((4, EXTENDED, LANES), BF16),
             jax.ShapeDtypeStruct(bands, BF16),
         ),
         in_specs=[far] * len(inputs) + [pl.BlockSpec(memory_space=pltpu.VMEM), smem, smem],
-        out_specs=(far, far, far),
+        out_specs=(far, far),
         scratch_shapes=[
             *copies, chunked, chunked, chunked, chunked,
             pltpu.VMEM((2, 64, LANES), F32), pltpu.VMEM((4, 64, LANES), F32),
-            pltpu.VMEM((4, 1088, LANES), BF16), pltpu.VMEM((512, 512), BF16),
-            pltpu.VMEM(early, F32), pltpu.VMEM(bands, BF16),
-            dma((len(inputs),)), dma((4,)), dma((4,)), dma((4,)), dma((2,)), dma((2,)), dma((3,)),
+            pltpu.VMEM((4, EXTENDED, LANES), BF16), pltpu.VMEM((512, 512), BF16),
+            pltpu.VMEM(bands, BF16),
+            dma((len(inputs) + 2,)), dma((4,)), dma((4,)), dma((4,)), dma((2,)), dma((2,)), dma((4,)),
             pltpu.SemaphoreType.REGULAR,
         ],
         compiler_params=pltpu.CompilerParams(
@@ -430,22 +427,22 @@
     )(*inputs, templates, drift_template, drift_reach)
 
 
-def correlate(rows, early, bands):
+def correlate(rows, bands):
     far = pl.BlockSpec(memory_space=pl.ANY)
     dma = pltpu.SemaphoreType.DMA
     powers = pl.pallas_call(
         correlate_kernel,
         name="correlate",
         out_shape=jax.ShapeDtypeStruct((2, LANES, 8, 8, LANES), F32),
-        in_specs=[far] * 3,
+        in_specs=[far] * 2,
         out_specs=far,
         scratch_shapes=[
             pltpu.VMEM(rows.shape, BF16), pltpu.VMEM(bands.shape, BF16),
-            *[pltpu.VMEM((2, LANES, 8, LANES), F32) for _ in range(6)],
-            dma, dma((DRIFTS // 2,)), dma((2,)), dma((6,)),
+            *[pltpu.VMEM((2, LANES, 8, LANES), F32) for _ in range(8)],
+            dma, dma((DRIFTS // 2,)), dma((8,)),
         ],
         compiler_params=pltpu.CompilerParams(vmem_limit_bytes=60 << 20),
-    )(rows, early, bands)
+    )(rows, bands)
     return powers.transpose(0, 3, 1, 2, 4).reshape(DRIFTS, LANES * ROWS)
 
 

time: 133 us -> 76.5 us (0.58)
  the two profiles are of different devices: /device:TPU:8 before, /device:TPU:1 now
where the time goes in v2:
time: 76.5 us; the launch traced here: 76.4 us
  Pallas kernels  76.2 us (100%)
    pallas_call x1, Pallas kernels, spectrum(): pl.pallas_call(spectrum_kernel, name='spectrum', out_shape=(jax.ShapeDtyp...  65.4 us
    pallas_call x1, Pallas kernels, correlate(): pl.pallas_call(correlate_kernel, name='correlate', out_shape=jax.ShapeDty...  10.8 us

profile of v2, /device:TPU:1, one launch (start us, length us, event | category | flops | bytes accessed | tf_op | source)
XLA Modules:
  0.0 76.4 jit_solution(11907315769205351328)
XLA Ops:
  0.0 65.4 %spectrum.1 = (bf16[4,1088,128]{2,1,0:T(8,128)(2,1)}, bf16[8,2,256,256]{3,2,1,0:T(8,128)(2,1)}) custom-call(f32[2,1024,128]{2,1,0:T(8,128)} %series_in.1, bf16[2,512,1024]{2,1,0:T(8,128)(2,1)} %constant.28.clone.column_hi_in, bf16[2,512,1024]{2,1,0:T(8,128)(2,1)} %constant.29.clone.column_lo_in, f32[2,2,512,128]{3,2,1,0:T(8,128)} %constant.30.clone.turn_in, ...), custom_call_target="tpu_custom_call" | custom-call | tf_op jit(solution)/shard_map/spectrum/pallas_call | solution.py:407
  65.4 10.8 %correlate.1 = f32[2,128,8,8,128]{4,3,2,1,0:T(8,128)} custom-call(bf16[4,1088,128]{2,1,0:T(8,128)(2,1)} %get-tuple-element.7.rows_in, bf16[8,2,256,256]{3,2,1,0:T(8,128)(2,1)} %get-tuple-element.8.bands_in), custom_call_target="tpu_custom_call" | custom-call | tf_op jit(solution)/shard_map/correlate/pallas_call | solution.py:433

commit v3 on v2

--- a/solution.py
+++ b/solution.py
@@ -187,6 +187,61 @@
     column_part(1)
     send_all(send_one, recv_one, 1, 1)
 
+    def row_part(real, imag):
+        wide = product((outer_hi[...], outer_lo[...]), split(jnp.concatenate([real, imag], axis=0)))
+        done = []
+        for e in range(2):
+            a, b = wide[:HALF, e * LANES : (e + 1) * LANES], wide[HALF:, e * LANES : (e + 1) * LANES]
+            turned = [a * twist[0] - b * twist[1], a * twist[1] + b * twist[0]]
+            done.append(
+                product_t((inner_hi[...], inner_lo[...]), split(jnp.concatenate(turned, axis=1)))
+            )
+        return done
+
+    def store(chunk, part, value, flip):
+        for h in range(2):
+            first = 4 * (1 - h if flip else h) + part
+            send_two[chunk, pl.ds(first, LANES, stride=8), :] = value[:, h * LANES : (h + 1) * LANES]
+
+    def store_direct(chunk, even, odd):
+        odd_real, odd_imag = odd[0:128], odd[128:256]
+        store(chunk, 0, even[0:128] + (join[0] * odd_real - join[1] * odd_imag), False)
+        store(chunk, 1, even[128:256] + (join[0] * odd_imag + join[1] * odd_real), False)
+
+    def store_mirrored(chunk, even, odd):
+        odd_real, odd_imag = odd[256:384], odd[384:512]
+        store(chunk, 2, even[256:384] - (join[2] * odd_real - join[3] * odd_imag), True)
+        store(chunk, 3, (join[2] * odd_imag + join[3] * odd_real) - even[384:512], True)
+
+    def arrived(chunk):
+        return [recv_one[chunk, pl.ds(s, HALF, stride=4), :] for s in range(4)]
+
+    def rows_of(chunk):
+        parts = arrived(chunk)
+        real = jnp.concatenate([parts[0], parts[2]], axis=1)
+        imag = jnp.concatenate([parts[1], parts[3]], axis=1)
+        if chunk == 0:
+            imag = imag * (me != 0).astype(F32)
+        even, odd = row_part(real, imag)
+        store_direct(chunk, even, odd)
+        store_mirrored(chunk, even, odd)
+
+    wait_all(send_one, recv_one, 0, recv_sem.at[0])
+    rows_of(0)
+
+    @pl.when(me == 0)
+    def _():
+        parts = arrived(0)
+        real = jnp.concatenate([parts[1] * middle[0, 0], parts[3] * middle[1, 0]], axis=1)
+        imag = jnp.concatenate([parts[1] * middle[0, 1], parts[3] * middle[1, 1]], axis=1)
+        even, odd = row_part(real, imag)
+        store_mirrored(0, even, odd)
+
+    send_all(send_two, bins, 0, 2)
+    wait_all(send_one, recv_one, 1, recv_sem.at[1])
+    rows_of(1)
+    send_all(send_two, bins, 1, 3)
+
     lane = lax.broadcasted_iota(jnp.int32, (1, LANES), 1)
     for d in range(DRIFTS):
         taps = templates[pl.ds(chosen[d], 1), :]
@@ -204,60 +259,6 @@
     bands_copy = pltpu.make_async_copy(bands, bands_out, out_sem.at[0])
     bands_copy.start()
 
-    def row_part(real, imag):
-        wide = product((outer_hi[...], outer_lo[...]), split(jnp.concatenate([real, imag], axis=0)))
-        done = []
-        for e in range(2):
-            a, b = wide[:HALF, e * LANES : (e + 1) * LANES], wide[HALF:, e * LANES : (e + 1) * LANES]
-            turned = [a * twist[0] - b * twist[1], a * twist[1] + b * twist[0]]
-            done.append(
-                product_t((inner_hi[...], inner_lo[...]), split(jnp.concatenate(turned, axis=1)))
-            )
-        return done
-
-    def store(chunk, part, value, flip):
-        for h in range(2):
-            first = 4 * (1 - h if flip else h) + part
-            send_two[chunk, pl.ds(first, LANES, stride=8), :] = value[:, h * LANES : (h + 1) * LANES]
-
-    def store_direct(chunk, even, odd):
-        odd_real, odd_imag = odd[0:128], odd[128:256]
-        store(chunk, 0, even[0:128] + (join[0] * odd_real - join[1] * odd_imag), False)
-        store(chunk, 1, even[128:256] + (join[0] * odd_imag + join[1] * odd_real), False)
-
-    def store_mirrored(chunk, even, odd):
-        odd_real, odd_imag = odd[256:384], odd[384:512]
-        store(chunk, 2, even[256:384] - (join[2] * odd_real - join[3] * odd_imag), True)
-        store(chunk, 3, (join[2] * odd_imag + join[3] * odd_real) - even[384:512], True)
-
-    def arrived(chunk):
-        return [recv_one[chunk, pl.ds(s, HALF, stride=4), :] for s in range(4)]
-
-    def rows_of(chunk):
-        parts = arrived(chunk)
-        real = jnp.concatenate([parts[0], parts[2]], axis=1)
-        imag = jnp.concatenate([parts[1], parts[3]], axis=1)
-        if chunk == 0:
-            imag = imag * (me != 0).astype(F32)
-        even, odd = row_part(real, imag)
-        store_direct(chunk, even, odd)
-        store_mirrored(chunk, even, odd)
-
-    wait_all(send_one, recv_one, 0, recv_sem.at[0])
-    rows_of(0)
-
-    @pl.when(me == 0)
-    def _():
-        parts = arrived(0)
-        real = jnp.concatenate([parts[1] * middle[0, 0], parts[3] * middle[1, 0]], axis=1)
-        imag = jnp.concatenate([parts[1] * middle[0, 1], parts[3] * middle[1, 1]], axis=1)
-        even, odd = row_part(real, imag)
-        store_mirrored(0, even, odd)
-
-    send_all(send_two, bins, 0, 2)
-    wait_all(send_one, recv_one, 1, recv_sem.at[1])
-    rows_of(1)
-    send_all(send_two, bins, 1, 3)
     wait_all(send_two, bins, 0, recv_sem.at[2])
 
     def halo_rows(side):
@@ -360,31 +361,36 @@
         return [jnp.concatenate([window(level, odd) for odd in range(2)], axis=0) for level in range(2)]
 
     low_lanes = lax.broadcasted_iota(jnp.int32, (LANES, LANES), 1) < TAPS
-    copies, pending = [], []
+    copies = []
     row_copy.wait()
     for copy in band_copies:
         copy.wait()
-    coming = windows_of(0)
-    for tile in range(8):
-        windows = coming
-        if tile < 7:
-            coming = windows_of(tile + 1)
-        flat = tiles[tile].reshape(2 * LANES * 8, LANES)
+    coming, following = windows_of(0), windows_of(1)
+    for half in range(4):
+        both = (2 * half, 2 * half + 1)
+        windows = [jnp.concatenate([first, second], axis=0) for first, second in zip(coming, following)]
+        if half < 3:
+            coming, following = windows_of(2 * half + 2), windows_of(2 * half + 3)
         for pair in range(DRIFTS // 2):
             response = product_t(windows, (bands[pair, 0], bands[pair, 1]))
             real, imag = response[:, :LANES], response[:, LANES:]
             power = real * real + imag * imag
-            even, odd = power[:LANES], power[LANES:]
-            first = jnp.where(low_lanes, even, pltpu.roll(odd, TAPS, 1))
-            second = jnp.where(low_lanes, pltpu.roll(even, TAPS, 1), odd)
-            for d, value in ((2 * pair, first), (2 * pair + 1, second)):
-                flat[pl.ds(d // 8 * LANES * 8 + d % 8, LANES, stride=8), :] = value
-        pending.append(pltpu.make_async_copy(tiles[tile], out.at[:, :, tile], out_sem.at[tile]))
-        if tile in (3, 6, 7):
-            for copy in pending:
-                copy.start()
-            copies += pending
-            pending = []
+            for tile in both:
+                flat = tiles[tile].reshape(2 * LANES * 8, LANES)
+                at = 2 * LANES * (tile % 2)
+                even, odd = power[at : at + LANES], power[at + LANES : at + 2 * LANES]
+                first = jnp.where(low_lanes, even, pltpu.roll(odd, TAPS, 1))
+                second = jnp.where(low_lanes, pltpu.roll(even, TAPS, 1), odd)
+                for d, value in ((2 * pair, first), (2 * pair + 1, second)):
+                    flat[pl.ds(d // 8 * LANES * 8 + d % 8, LANES, stride=8), :] = value
+            if pair % 4 == 3:
+                for tile in both:
+                    block = pair // 4
+                    copy = pltpu.make_async_copy(
+                        tiles[tile].at[block], out.at[block, :, tile], out_sem.at[2 * tile + block]
+                    )
+                    copy.start()
+                    copies.append(copy)
     for copy in copies:
         copy.wait()
 
@@ -439,7 +445,7 @@
         scratch_shapes=[
             pltpu.VMEM(rows.shape, BF16), pltpu.VMEM(bands.shape, BF16),
             *[pltpu.VMEM((2, LANES, 8, LANES), F32) for _ in range(8)],
-            dma, dma((DRIFTS // 2,)), dma((8,)),
+            dma, dma((DRIFTS // 2,)), dma((16,)),
         ],
         compiler_params=pltpu.CompilerParams(vmem_limit_bytes=60 << 20),
     )(rows, bands)

time: 76.5 us -> 75.5 us (0.987)
  Pallas kernels: 76.2 us -> 75.2 us
    pallas_call x1, Pallas kernels: 10.8 us -> 9.79 us  [correlate(): pl.pallas_call(correlate_kernel, name='correlate', out_shape=jax.ShapeDty...]
where the time goes in v3:
time: 75.5 us; the launch traced here: 75.4 us
  Pallas kernels  75.2 us (100%)
    pallas_call x1, Pallas kernels, spectrum(): pl.pallas_call(spectrum_kernel, name='spectrum', out_shape=(jax.ShapeDtyp...  65.4 us
    pallas_call x1, Pallas kernels, correlate(): pl.pallas_call(correlate_kernel, name='correlate', out_shape=jax.ShapeDty...  9.79 us

profile of v3, /device:TPU:1, one launch (start us, length us, event | category | flops | bytes accessed | tf_op | source)
XLA Modules:
  0.0 75.4 jit_solution(9807677254436397976)
XLA Ops:
  0.0 65.4 %spectrum.1 = (bf16[4,1088,128]{2,1,0:T(8,128)(2,1)}, bf16[8,2,256,256]{3,2,1,0:T(8,128)(2,1)}) custom-call(f32[2,1024,128]{2,1,0:T(8,128)} %series_in.1, bf16[2,512,1024]{2,1,0:T(8,128)(2,1)} %constant.28.clone.column_hi_in, bf16[2,512,1024]{2,1,0:T(8,128)(2,1)} %constant.29.clone.column_lo_in, f32[2,2,512,128]{3,2,1,0:T(8,128)} %constant.30.clone.turn_in, ...), custom_call_target="tpu_custom_call" | custom-call | tf_op jit(solution)/shard_map/spectrum/pallas_call | solution.py:413
  65.4 9.8 %correlate.1 = f32[2,128,8,8,128]{4,3,2,1,0:T(8,128)} custom-call(bf16[4,1088,128]{2,1,0:T(8,128)(2,1)} %get-tuple-element.7.rows_in, bf16[8,2,256,256]{3,2,1,0:T(8,128)(2,1)} %get-tuple-element.8.bands_in), custom_call_target="tpu_custom_call" | custom-call | tf_op jit(solution)/shard_map/correlate/pallas_call | solution.py:439

commit v4 on v3

--- a/solution.py
+++ b/solution.py
@@ -363,9 +363,9 @@
     low_lanes = lax.broadcasted_iota(jnp.int32, (LANES, LANES), 1) < TAPS
     copies = []
     row_copy.wait()
+    coming, following = windows_of(0), windows_of(1)
     for copy in band_copies:
         copy.wait()
-    coming, following = windows_of(0), windows_of(1)
     for half in range(4):
         both = (2 * half, 2 * half + 1)
         windows = [jnp.concatenate([first, second], axis=0) for first, second in zip(coming, following)]

time: 75.5 us -> 75.6 us (level)
  no operation moved by 1% of the time
where the time goes in v4:
time: 75.6 us; the launch traced here: 75.5 us
  Pallas kernels  75.4 us (100%)
    pallas_call x1, Pallas kernels, spectrum(): pl.pallas_call(spectrum_kernel, name='spectrum', out_shape=(jax.ShapeDtyp...  65.4 us
    pallas_call x1, Pallas kernels, correlate(): pl.pallas_call(correlate_kernel, name='correlate', out_shape=jax.ShapeDty...  9.96 us

profile of v4, /device:TPU:1, one launch (start us, length us, event | category | flops | bytes accessed | tf_op | source)
XLA Modules:
  0.0 75.5 jit_solution(18160313459458518885)
XLA Ops:
  0.0 65.4 %spectrum.1 = (bf16[4,1088,128]{2,1,0:T(8,128)(2,1)}, bf16[8,2,256,256]{3,2,1,0:T(8,128)(2,1)}) custom-call(f32[2,1024,128]{2,1,0:T(8,128)} %series_in.1, bf16[2,512,1024]{2,1,0:T(8,128)(2,1)} %constant.28.clone.column_hi_in, bf16[2,512,1024]{2,1,0:T(8,128)(2,1)} %constant.29.clone.column_lo_in, f32[2,2,512,128]{3,2,1,0:T(8,128)} %constant.30.clone.turn_in, ...), custom_call_target="tpu_custom_call" | custom-call | tf_op jit(solution)/shard_map/spectrum/pallas_call | solution.py:413
  65.4 10.0 %correlate.1 = f32[2,128,8,8,128]{4,3,2,1,0:T(8,128)} custom-call(bf16[4,1088,128]{2,1,0:T(8,128)(2,1)} %get-tuple-element.7.rows_in, bf16[8,2,256,256]{3,2,1,0:T(8,128)(2,1)} %get-tuple-element.8.bands_in), custom_call_target="tpu_custom_call" | custom-call | tf_op jit(solution)/shard_map/correlate/pallas_call | solution.py:439
